TPU v7x, 256 devices: a whole 4x4x8 slice. The times are simulated.
256 devices in a mesh: dp: 64 (over z_hi, x, y), tensor: 4 (over z_lo, core).
Axes of the slice: x: 4, y: 4, z: 8 (z_hi: 4, z_lo: 2; z = z_hi * 2 + z_lo), core: 2. Of those that a mesh axis runs over, the one named last changes fastest.
Arguments:
- page_acts: bfloat16 [32768, 5120], P('dp', 'tensor'), may hold values from -6 to 6
- out_grad_key: bfloat16 [32768, 1024], P('dp', 'tensor'), may hold values from -6 to 6
- out_grad_value: bfloat16 [32768, 1024], P('dp', 'tensor'), may hold values from -6 to 6
- key_weight: bfloat16 [5120, 1024], P(None, 'tensor'), may hold values from -0.078125 to 0.078125
- value_weight: bfloat16 [5120, 1024], P(None, 'tensor'), may hold values from -0.078125 to 0.078125
Outputs:
- grad_input: bfloat16 [32768, 5120], P('dp', 'tensor')
- fisher_key: float32 [5120, 1024], P('dp', 'tensor')
- fisher_value: float32 [5120, 1024], P('dp', 'tensor')
All inputs are finite; a program needn't handle non-finite values.
Results may differ from a plain program's by a relative error of at most 0.001.
Values may be sent and summed in bfloat16 or wider, within the bound.
No kernel may reach another device: no remote copies, remote signals or barrier semaphores. Data moves between devices by JAX's collectives and lax.ppermute only.
A program may use at most 128 MiB of HBM per device.

v0:
```python
import functools

import jax
import jax.numpy as jnp
from jax import lax
from jax.experimental import pallas as pl
from jax.experimental.pallas import tpu as pltpu
from jax.sharding import PartitionSpec as P

PAGE = 512
AXES = ("dp", "tensor")
X, Y, ZH, T = 4, 4, 4, 4
BLOCKS = X * Y
HIGH = 16384.0
TAIL = 16
ORDER = ((0, 3, 1, 2), (0, 1, 3, 2))
FIRST, SECOND = (1, 3), (3, 1)
ADD_COST = 4 << 30
VMEM = pl.BlockSpec(memory_space=pltpu.VMEM)
ANY = pl.BlockSpec(memory_space=pl.ANY)


def device(zh, x, y, t):
    return (zh * BLOCKS + x * Y + y) * T + t


def devices():
    return [(zh, x, y, t) for zh in range(ZH) for x in range(X) for y in range(Y) for t in range(T)]


def swap(first_axis, distance):
    pairs = []
    for zh, x, y, t in devices():
        along_x = (t % 2 == 0) == first_axis
        there = (x ^ distance, y) if along_x else (x, y ^ distance)
        pairs.append((device(zh, x, y, t), device(zh, *there, t)))
    return pairs


def tensor_swap(flip):
    return [(device(zh, x, y, t), device(zh, x, y, t ^ flip)) for zh, x, y, t in devices()]


def outer_z_swap():
    pairs = []
    for zh, x, y, t in devices():
        z = zh * 2 + t // 2
        there = (z + 1 if z % 2 else z - 1) % (2 * ZH)
        pairs.append((device(zh, x, y, t), device(there // 2, x, y, (there % 2) * 2 + t % 2)))
    return pairs


def owner_step(k):
    return [(device(zh, x, y, t), device(t, x, y, zh ^ k)) for zh, x, y, t in devices()]


def send(value, pairs):
    return lax.ppermute(value, AXES, pairs)


def local_call(kernel, out_shape, operands, specs=None, outs=VMEM, scratch=(), flops=0, limit=12):
    return pl.pallas_call(
        kernel,
        in_specs=specs or [VMEM] * len(operands),
        out_specs=[outs] * len(out_shape),
        out_shape=list(out_shape),
        scratch_shapes=list(scratch),
        compiler_params=pltpu.CompilerParams(vmem_limit_bytes=limit << 20),
        cost_estimate=pl.CostEstimate(flops=flops, bytes_accessed=0, transcendentals=0),
    )(*operands)


def shape(rows, columns, dtype=jnp.float32):
    return jax.ShapeDtypeStruct((rows, columns), dtype)


def join_kernel(left, right, out, sems):
    width = left.shape[1]
    copies = [
        pltpu.make_async_copy(src, out.at[:, pl.ds(h * width, width)], sems.at[h])
        for h, src in enumerate((left, right))
    ]
    for copy in copies:
        copy.start()
    for copy in copies:
        copy.wait()


def join(left, right):
    rows, width = left.shape
    out = [shape(rows, 2 * width, left.dtype)]
    sems = [pltpu.SemaphoreType.DMA((2,))]
    return local_call(join_kernel, out, (left, right), [ANY] * 2, scratch=sems, limit=2)[0]


def weights_kernel(kw_ref, vw_ref, w0, w1, w2, w3, sems):
    rows, width = w0.shape[0], kw_ref.shape[1]
    t = lax.axis_index("tensor")
    copies = []
    for q, out in ((2, w2), (3, w3), (1, w1), (0, w0)):
        picked = pl.ds(pl.multiple_of((t ^ q) * rows, rows), rows)
        for h, src in enumerate((kw_ref, vw_ref)):
            copies.append(
                pltpu.make_async_copy(
                    src.at[picked, :], out.at[:, pl.ds(h * width, width)], sems.at[2 * q + h]
                )
            )
    for copy in copies:
        copy.start()
    for copy in copies:
        copy.wait()


def pick_weights(kw, vw):
    rows, width = kw.shape[0] // T, kw.shape[1]
    out = [shape(rows, 2 * width, kw.dtype)] * 4
    sems = [pltpu.SemaphoreType.DMA((8,))]
    return local_call(weights_kernel, out, (kw, vw), [ANY] * 2, ANY, sems, limit=2)


def turn_kernel(a_ref, at0_ref, at1_ref, turned):
    rows = a_ref.shape[1]
    dp, t = lax.axis_index("dp"), lax.axis_index("tensor")
    place = dp & (BLOCKS - 1)
    along_x = (t & 1) == 0
    for j in range(0, rows, 128):
        turned[j : j + 128, :] = a_ref[:, j : j + 128].T
    size = rows // BLOCKS
    for out, order in ((at0_ref, ORDER[0]), (at1_ref, ORDER[1])):
        for p1, e1 in enumerate(order):
            for e2 in range(4):
                block = place ^ jnp.where(along_x, e1 * Y + e2, e2 * Y + e1)
                start = pl.multiple_of(block * size, 16)
                to = (p1 * 4 + e2) * size
                out[to : to + size, :] = turned[pl.ds(start, size), :]


def turn(a):
    tokens, rows = a.shape
    out = [shape(rows, tokens, a.dtype)] * 2
    return local_call(turn_kernel, out, (a,), scratch=[pltpu.VMEM((rows, tokens), a.dtype)])


def exponent_of(bound):
    return jnp.clip(jnp.floor(jnp.log2(HIGH / jnp.maximum(bound, 1e-30))), -60.0, 100.0)


def unit_of(exponent):
    return 1.0 / jnp.exp2(exponent)


def fill(out, at, count, row):
    out[at : at + count, :] = jnp.broadcast_to(row, (count, out.shape[1]))


def squares_kernel(at0, at1, g0, g1, keep0, bound0, out0, keep1, bound1, out1):
    half, width = keep0.shape[0], g0.shape[1] // 2
    step = half // 2
    streams = ((at0, 0, keep0, bound0, out0), (at1, width, keep1, bound1, out1))
    for moved in (True, False):
        for at, lo, keep, bound, out in streams:
            tops = [jnp.zeros((8, width), jnp.float32)] * 2
            to, base = (out, half) if moved else (keep, 0)
            for r in range(0, half, step):
                rows = at[base + r : base + r + step, :]
                for h, g in enumerate((g0, g1)):
                    grad = jnp.dot(rows, g[:, lo : lo + width], preferred_element_type=jnp.float32)
                    grad = grad * grad
                    to[r : r + step, h * width : (h + 1) * width] = grad
                    tops[h] = jnp.maximum(tops[h], jnp.max(grad.reshape(-1, 8, width), axis=0))
            top = jnp.concatenate([jnp.max(top, axis=0, keepdims=True) for top in tops], axis=1)
            if moved:
                exponent = exponent_of(top)
                scale = jnp.exp2(exponent)
                for r in range(0, half, 80):
                    out[r : r + 80, :] = out[r : r + 80, :] * scale
                fill(out, half, TAIL, exponent)
            else:
                bound[...] = top


def squares(at0, at1, g0, g1):
    rows, width = at0.shape[0], g0.shape[1]
    out = [shape(rows // 2, width), shape(1, width), shape(rows // 2 + TAIL, width)] * 2
    out = local_call(squares_kernel, out, (at0, at1, g0, g1))
    return out[:3], out[3:]


def add_kernel(keep0, bound0, got0, keep1, bound1, got1, sum0, top0, sum1, top1):
    rows = keep0.shape[0]
    for keep, bound, got, total, top in (
        (keep0, bound0, got0, sum0, top0),
        (keep1, bound1, got1, sum1, top1),
    ):
        unit = unit_of(got[rows : rows + 1, :])
        top[...] = bound[...] + HIGH * unit
        for r in range(0, rows, 80):
            total[r : r + 80, :] = keep[r : r + 80, :] + got[r : r + 80, :] * unit


def add(*operands):
    rows, width = operands[0].shape
    out = local_call(add_kernel, [shape(rows, width), shape(1, width)] * 2, operands, flops=ADD_COST)
    return out[:2], out[2:]


def halve_kernel(near, near_bound, keep, bound, got, new0, new1, bounds, out):
    rows = keep.shape[0]
    half = rows // 2
    unit = unit_of(got[rows : rows + 1, :])
    tops = (near_bound[...], bound[...] + HIGH * unit)
    exponents = [exponent_of(top) for top in tops]
    scales = [jnp.exp2(exponent) for exponent in exponents]
    for r in range(half, rows, 80):
        to = r - half
        out[to : to + 80, :] = near[r : r + 80, :] * scales[0]
        value = keep[r : r + 80, :] + got[r : r + 80, :] * unit
        out[r : r + 80, :] = value * scales[1]
    for r in range(0, half, 80):
        new0[r : r + 80, :] = near[r : r + 80, :]
        new1[r : r + 80, :] = keep[r : r + 80, :] + got[r : r + 80, :] * unit
    for h in range(2):
        bounds[h : h + 1, :] = tops[h]
        fill(out, rows + h * (TAIL // 2), TAIL // 2, exponents[h])


def halve(*operands):
    rows, width = operands[0].shape
    out = [shape(rows // 2, width)] * 2 + [shape(2, width), shape(rows + TAIL, width)]
    return local_call(halve_kernel, out, operands)


def share_kernel(near0, far0, bounds0, got0, near1, far1, bounds1, got1, own, bounds, *outs):
    rows = near0.shape[0]
    size, each = rows // 4, TAIL // 4
    streams = ((near0, far0, bounds0, got0), (near1, far1, bounds1, got1))
    for s, (near, far, kept_bounds, got) in enumerate(streams):
        for h, keep in enumerate((near, far)):
            p = 2 * s + h
            tail = 2 * rows + h * (TAIL // 2)
            unit = unit_of(got[tail : tail + 1, :])
            top = kept_bounds[h : h + 1, :] + HIGH * unit
            exponent = exponent_of(top)
            scale = jnp.exp2(exponent)
            bounds[p : p + 1, :] = top
            for e, out in ((1, outs[0]), (3, outs[2]), (2, outs[1]), (0, own)):
                at = e * size
                arrived = got[h * rows + at : h * rows + at + size, :]
                value = keep[at : at + size, :] + arrived * unit
                out[p * size : (p + 1) * size, :] = value if e == 0 else value * scale
            for out in outs:
                fill(out, 4 * size + p * each, each, exponent)


def share(*operands):
    rows, width = operands[0].shape
    out = [shape(rows, width), shape(4, width)] + [shape(rows + TAIL, width)] * 3
    own, bounds, *messages = local_call(share_kernel, out, operands)
    return own, bounds, messages


def spread_kernel(own, bounds, got1, got2, got3, *refs):
    outs, staged = refs[:T], refs[T]
    rows, width = own.shape[0], own.shape[1] // 2
    size = rows // 4
    for p in range(4):
        tail = rows + p * (TAIL // 4)
        value, top = own[p * size : (p + 1) * size, :], bounds[p : p + 1, :]
        for got in (got1, got2, got3):
            unit = unit_of(got[tail : tail + 1, :])
            value = value + got[p * size : (p + 1) * size, :] * unit
            top = top + HIGH * unit
        exponent = exponent_of(top)
        value = value * jnp.exp2(exponent)
        s, h = p // 2, p % 2
        for i in range(2):
            q, columns = 2 * h + i, slice(i * width, (i + 1) * width)
            staged[q, s * size : (s + 1) * size, :] = value[:, columns]
            row = jnp.broadcast_to(exponent[:, columns], (TAIL // 2, width))
            to = 2 * size + s * (TAIL // 2)
            staged[q, to : to + TAIL // 2, :] = row
    distance = lax.axis_index("tensor") ^ (lax.axis_index("dp") >> 4)
    for k, out in enumerate(outs):
        out[...] = staged[distance ^ k]


def spread(*operands):
    rows, width = operands[0].shape[0] // 2 + TAIL, operands[0].shape[1] // 2
    scratch = [pltpu.VMEM((T, rows, width), jnp.float32)]
    return local_call(spread_kernel, [shape(rows, width)] * T, operands, scratch=scratch)


def total_kernel(factor, *refs):
    gots, outs = refs[:-2], refs[-2:]
    size = outs[0].shape[0]
    for s, out in enumerate(outs):
        tail = 2 * size + s * (TAIL // 2)
        total = 0.0
        for got in gots:
            unit = factor / jnp.exp2(got[tail : tail + 1, :])
            total = total + got[s * size : (s + 1) * size, :] * unit
        out[...] = total


def total(gots, factor):
    rows, width = (gots[0].shape[0] - TAIL) // 2, gots[0].shape[1]
    return local_call(functools.partial(total_kernel, factor), [shape(rows, width)] * 2, gots)


def right_product(left, right):
    return lax.dot_general(
        left, right, (((1,), (1,)), ((), ())), preferred_element_type=jnp.float32
    )


def narrow(values):
    return [value.astype(jnp.float16) for value in values]


def wide(values):
    return [value.astype(jnp.float32) for value in values]


def per_device(page_acts, out_grad_key, out_grad_value, key_weight, value_weight):
    g0 = join(out_grad_key, out_grad_value)
    g2 = send(g0, tensor_swap(2))
    g1 = send(g0, tensor_swap(1))
    at = turn(page_acts)

    near = squares(*at, g0, g1)
    out = narrow([stream[2] for stream in near])
    near_got = wide([send(out[s], swap(True, FIRST[s])) for s in range(2)])
    kw, vw, _ = lax.optimization_barrier((key_weight, value_weight, out))
    w0, w1, w2, w3 = pick_weights(kw, vw)
    g2, _ = lax.optimization_barrier((g2, w2))
    g3 = send(g2, tensor_swap(1))
    near = add(*near[0][:2], near_got[0], *near[1][:2], near_got[1])
    far = squares(*at, g2, g3)
    out = narrow([stream[2] for stream in far])
    out, near, w2, w3 = lax.optimization_barrier((out, near, w2, w3))
    far_got = [send(out[s], swap(True, FIRST[s])) for s in range(2)]
    w1 = send(w1, tensor_swap(1))
    w1, w2, w3 = lax.optimization_barrier((w1, w2, w3))
    w2 = send(w2, outer_z_swap())
    w3 = send(w3, tensor_swap(3))
    far_got = wide(far_got)

    streams = [halve(*near[s], *far[s][:2], far_got[s]) for s in range(2)]
    out = narrow([stream[3] for stream in streams])
    got = [send(out[s], swap(True, SECOND[s])) for s in range(2)]
    grad_input = right_product(g0, w0) + right_product(g1, w1)
    got, grad_input = lax.optimization_barrier((wide(got), grad_input))
    own, bounds, out = share(*streams[0][:3], got[0], *streams[1][:3], got[1])
    out = narrow(out)
    one, three, two = (send(out[e - 1], swap(False, e)) for e in (1, 3, 2))
    got = [one, two, three]
    got, w2, w3 = lax.optimization_barrier((wide(got), w2, w3))
    outs = spread(own, bounds, *got)
    w1, w2, w3, _ = lax.optimization_barrier((w1, w2, w3, outs))
    got = [send(out, owner_step(k)) for k, out in enumerate(narrow(outs))]
    fisher_key, fisher_value = total(wide(got), 1.0 / (lax.axis_size("dp") * PAGE))

    grad_input = grad_input + (right_product(g2, w2) + right_product(g3, w3))
    return grad_input.astype(jnp.bfloat16), fisher_key, fisher_value


def solution(mesh):
    in_specs = (
        P("dp", "tensor"),
        P("dp", "tensor"),
        P("dp", "tensor"),
        P(None, "tensor"),
        P(None, "tensor"),
    )
    out_specs = (P("dp", "tensor"), P("dp", "tensor"), P("dp", "tensor"))
    return jax.shard_map(
        per_device, mesh=mesh, in_specs=in_specs, out_specs=out_specs, check_vma=False
    )
```

profile of v0, /device:TPU:32, one launch (start us, length us, event | category | flops | bytes accessed | tf_op | source)
XLA Modules:
  0.0 79.8 jit_solution(8173338706233627034)
XLA Ops:
  0.6 0.9 %copy-done.3 = bf16[512,256]{1,0:T(8,128)(2,1)S(1)} copy-done((bf16[512,256]{1,0:T(8,128)(2,1)S(1)}, bf16[512,256]{1,0:T(8,128)(2,1)}, u32[]{:S(2)}) %copy-start.3) | copy-done | bytes 262168
  1.6 0.9 %copy-done.4 = bf16[512,256]{1,0:T(8,128)(2,1)S(1)} copy-done((bf16[512,256]{1,0:T(8,128)(2,1)S(1)}, bf16[512,256]{1,0:T(8,128)(2,1)}, u32[]{:S(2)}) %copy-start.4) | copy-done | bytes 262168
  2.7 1.9 %collective-permute-start = (bf16[512,512]{1,0:T(8,128)(2,1)S(1)}, bf16[512,512]{1,0:T(8,128)(2,1)S(1)}, u32[]{:S(2)}, u32[]{:S(2)}) collective-permute-start(bf16[512,512]{1,0:T(8,128)(2,1)S(1)} %shard_map.77.g0), channel_id=1, source_target_pairs={{0,2},{1,3},{2,0},{3,1},{4,6},{5,7},{6,4},{7,5},{8,10},{9,11},{10,... | collective-permute-start | bytes 1572872 | tf_op jit(solution)/shard_map/ppermute | solution.py:58
  4.6 1.3 %copy-done.2 = bf16[512,1280]{1,0:T(8,128)(2,1)S(1)} copy-done((bf16[512,1280]{1,0:T(8,128)(2,1)S(1)}, bf16[512,1280]{1,0:T(8,128)(2,1)}, u32[]{:S(2)}) %copy-start.2) | copy-done | bytes 1310744
  6.5 1.9 %shard_map.78 = (f32[640,512]{1,0:T(8,128)S(1)}, f32[1,512]{1,0:T(1,128)S(1)}, f32[656,512]{1,0:T(8,128)S(1)}, f32[640,512]{1,0:T(8,128)S(1)}, f32[1,512]{1,0:T(1,128)S(1)}, /*index=5*/f32[656,512]{1,0:T(8,128)S(1)}) custom-call(bf16[1280,512]{1,0:T(8,128)(2,1)S(1)} %get-tuple-element.68.at0, bf16[1280,512]{1,0:T(8,128)(2,1)S(1)} %get-tuple-element.69.at1, ...), custom_call_target="tpu_custom_call" | custom-call | tf_op jit(solution)/shard_map/pallas_call | solution.py:62
  8.5 1.1 %collective-permute-start.4 = (f16[656,512]{1,0:T(8,128)(2,1)S(1)}, f16[656,512]{1,0:T(8,128)(2,1)S(1)}, u32[]{:S(2)}, u32[]{:S(2)}) collective-permute-start(f16[656,512]{1,0:T(8,128)(2,1)S(1)} %convert_element_type.82), channel_id=1, source_target_pairs={{0,48},{1,13},{2,50},{3,15},{4,52},{5,9},{6,54},{7,11},{8,56},{9,5... | collective-permute-start | bytes 2015240 | tf_op jit(solution)/shard_map/ppermute | solution.py:58
  10.6 6.5 %collective-permute-done.g0 = bf16[512,512]{1,0:T(8,128)(2,1)S(1)} collective-permute-done((bf16[512,512]{1,0:T(8,128)(2,1)S(1)}, bf16[512,512]{1,0:T(8,128)(2,1)S(1)}, u32[]{:S(2)}, u32[]{:S(2)}) %collective-permute-start) | collective-permute-done | bytes 524320 | tf_op jit(solution)/shard_map/ppermute | solution.py:58
  17.6 1.4 %collective-permute-done.2.g1 = bf16[512,512]{1,0:T(8,128)(2,1)S(1)} collective-permute-done((bf16[512,512]{1,0:T(8,128)(2,1)S(1)}, bf16[512,512]{1,0:T(8,128)(2,1)S(1)}, u32[]{:S(2)}, u32[]{:S(2)}) %collective-permute-start.2) | collective-permute-done | bytes 524320 | tf_op jit(solution)/shard_map/ppermute | solution.py:58
  19.0 1.8 %shard_map.80 = (f32[640,512]{1,0:T(8,128)S(1)}, f32[1,512]{1,0:T(1,128)S(1)}, f32[656,512]{1,0:T(8,128)S(1)}, f32[640,512]{1,0:T(8,128)S(1)}, f32[1,512]{1,0:T(1,128)S(1)}, /*index=5*/f32[656,512]{1,0:T(8,128)S(1)}) custom-call(bf16[1280,512]{1,0:T(8,128)(2,1)S(1)} %get-tuple-element.68.at0, bf16[1280,512]{1,0:T(8,128)(2,1)S(1)} %get-tuple-element.69.at1, ...), custom_call_target="tpu_custom_call" | custom-call | tf_op jit(solution)/shard_map/pallas_call | solution.py:62
  21.8 1.5 %collective-permute-start.5 = (f16[656,512]{1,0:T(8,128)(2,1)S(1)}, f16[656,512]{1,0:T(8,128)(2,1)S(1)}, u32[]{:S(2)}, u32[]{:S(2)}) collective-permute-start(f16[656,512]{1,0:T(8,128)(2,1)S(1)} %convert_element_type.83), channel_id=1, source_target_pairs={{0,16},{1,5},{2,18},{3,7},{4,20},{5,1},{6,22},{7,3},{8,24},{9,13},... | collective-permute-start | bytes 2015240 | tf_op jit(solution)/shard_map/ppermute | solution.py:58
  23.3 2.1 %collective-permute-start.7 = (f16[656,512]{1,0:T(8,128)(2,1)S(1)}, f16[656,512]{1,0:T(8,128)(2,1)S(1)}, u32[]{:S(2)}, u32[]{:S(2)}) collective-permute-start(f16[656,512]{1,0:T(8,128)(2,1)S(1)} %convert_element_type.84), channel_id=1, source_target_pairs={{0,48},{1,13},{2,50},{3,15},{4,52},{5,9},{6,54},{7,11},{8,56},{9,5... | collective-permute-start | bytes 2015240 | tf_op jit(solution)/shard_map/ppermute | solution.py:58
  25.4 2.1 %collective-permute-start.13 = (bf16[1280,512]{1,0:T(8,128)(2,1)S(1)}, bf16[1280,512]{1,0:T(8,128)(2,1)S(1)}, u32[]{:S(2)}, u32[]{:S(2)}) collective-permute-start(bf16[1280,512]{1,0:T(8,128)(2,1)S(1)} %get-tuple-element.116), channel_id=1, source_target_pairs={{0,194},{1,195},{2,64},{3,65},{4,198},{5,199},{6,68},{7,69},{8,202... | collective-permute-start | bytes 3932168 | tf_op jit(solution)/shard_map/ppermute | solution.py:58
  27.5 3.0 %collective-permute-start.14 = (bf16[1280,512]{1,0:T(8,128)(2,1)S(1)}, bf16[1280,512]{1,0:T(8,128)(2,1)S(1)}, u32[]{:S(2)}, u32[]{:S(2)}) collective-permute-start(bf16[1280,512]{1,0:T(8,128)(2,1)S(1)} %get-tuple-element.117), channel_id=1, source_target_pairs={{0,3},{1,2},{2,1},{3,0},{4,7},{5,6},{6,5},{7,4},{8,11},{9,10},{10,... | collective-permute-start | bytes 3932168 | tf_op jit(solution)/shard_map/ppermute | solution.py:58
  30.5 2.2 %collective-permute-done.5 = f16[656,512]{1,0:T(8,128)(2,1)S(1)} collective-permute-done((f16[656,512]{1,0:T(8,128)(2,1)S(1)}, f16[656,512]{1,0:T(8,128)(2,1)S(1)}, u32[]{:S(2)}, u32[]{:S(2)}) %collective-permute-start.5) | collective-permute-done | bytes 671776 | tf_op jit(solution)/shard_map/ppermute | solution.py:58
  33.2 2.8 %collective-permute-start.6 = (f16[656,512]{1,0:T(8,128)(2,1)S(1)}, f16[656,512]{1,0:T(8,128)(2,1)S(1)}, u32[]{:S(2)}, u32[]{:S(2)}) collective-permute-start(f16[656,512]{1,0:T(8,128)(2,1)S(1)} %convert_element_type.88), channel_id=1, source_target_pairs={{0,48},{1,13},{2,50},{3,15},{4,52},{5,9},{6,54},{7,11},{8,56},{9,5... | collective-permute-start | bytes 2015240 | tf_op jit(solution)/shard_map/ppermute | solution.py:58
  38.0 0.9 %convolution_add_fusion.1 = f32[512,1280]{1,0:T(8,128)S(1)} fusion(f32[512,1280]{1,0:T(8,128)S(1)} %fusion, bf16[512,512]{1,0:T(8,128)(2,1)S(1)} %collective-permute-done.1.g1, bf16[1280,512]{1,0:T(8,128)(2,1)S(1)} %collective-permute-done.9), kind=kOutput, calls=%fused_computation.1 | convolution fusion | flops 671744000 | bytes 7077888 | tf_op jit(solution)/shard_map/dot_general | solution.py:311
  38.8 6.5 %collective-permute-done.6 = f16[656,512]{1,0:T(8,128)(2,1)S(1)} collective-permute-done((f16[656,512]{1,0:T(8,128)(2,1)S(1)}, f16[656,512]{1,0:T(8,128)(2,1)S(1)}, u32[]{:S(2)}, u32[]{:S(2)}) %collective-permute-start.6) | collective-permute-done | bytes 671776 | tf_op jit(solution)/shard_map/ppermute | solution.py:58
  45.5 2.1 %collective-permute-done.8 = f16[656,512]{1,0:T(8,128)(2,1)S(1)} collective-permute-done((f16[656,512]{1,0:T(8,128)(2,1)S(1)}, f16[656,512]{1,0:T(8,128)(2,1)S(1)}, u32[]{:S(2)}, u32[]{:S(2)}) %collective-permute-start.8) | collective-permute-done | bytes 671776 | tf_op jit(solution)/shard_map/ppermute | solution.py:58
  48.3 3.1 %collective-permute-start.12 = (f16[336,512]{1,0:T(8,128)(2,1)S(1)}, f16[336,512]{1,0:T(8,128)(2,1)S(1)}, u32[]{:S(2)}, u32[]{:S(2)}) collective-permute-start(f16[336,512]{1,0:T(8,128)(2,1)S(1)} %convert_element_type.97), channel_id=1, source_target_pairs={{0,12},{1,49},{2,14},{3,51},{4,8},{5,53},{6,10},{7,55},{8,4},{9,57... | collective-permute-start | bytes 1032200 | tf_op jit(solution)/shard_map/ppermute | solution.py:58
  52.6 7.9 %collective-permute-done.12 = f16[336,512]{1,0:T(8,128)(2,1)S(1)} collective-permute-done((f16[336,512]{1,0:T(8,128)(2,1)S(1)}, f16[336,512]{1,0:T(8,128)(2,1)S(1)}, u32[]{:S(2)}, u32[]{:S(2)}) %collective-permute-start.12) | collective-permute-done | bytes 344096 | tf_op jit(solution)/shard_map/ppermute | solution.py:58
  61.9 3.2 %collective-permute-start.18 = (f16[176,256]{1,0:T(8,128)(2,1)S(1)}, f16[176,256]{1,0:T(8,128)(2,1)S(1)}, u32[]{:S(2)}, u32[]{:S(2)}) collective-permute-start(f16[176,256]{1,0:T(8,128)(2,1)S(1)} %convert_element_type.106), channel_id=1, source_target_pairs={{0,3},{1,67},{2,131},{3,195},{4,7},{5,71},{6,135},{7,199},{8,11},{... | collective-permute-start | bytes 270344 | tf_op jit(solution)/shard_map/ppermute | solution.py:58
  65.1 3.2 %collective-permute-start.17 = (f16[176,256]{1,0:T(8,128)(2,1)S(1)}, f16[176,256]{1,0:T(8,128)(2,1)S(1)}, u32[]{:S(2)}, u32[]{:S(2)}) collective-permute-start(f16[176,256]{1,0:T(8,128)(2,1)S(1)} %convert_element_type.104), channel_id=1, source_target_pairs={{0,2},{1,66},{2,130},{3,194},{4,6},{5,70},{6,134},{7,198},{8,10},{... | collective-permute-start | bytes 270344 | tf_op jit(solution)/shard_map/ppermute | solution.py:58
  68.4 7.6 %collective-permute-start.15 = (f16[176,256]{1,0:T(8,128)(2,1)S(1)}, f16[176,256]{1,0:T(8,128)(2,1)S(1)}, u32[]{:S(2)}, u32[]{:S(2)}) collective-permute-start(f16[176,256]{1,0:T(8,128)(2,1)S(1)} %convert_element_type.100), channel_id=1, source_target_pairs={{0,0},{1,64},{2,128},{3,192},{4,4},{5,68},{6,132},{7,196},{8,8},{9... | collective-permute-start | bytes 270344 | tf_op jit(solution)/shard_map/ppermute | solution.py:58
  77.7 1.3 %add_convert_fusion = bf16[512,1280]{1,0:T(8,128)(2,1)} fusion(f32[512,1280]{1,0:T(8,128)S(1)} %convolution_add_fusion.1, f32[512,1280]{1,0:T(8,128)S(1)} %convolution_add_fusion), kind=kLoop, calls=%fused_computation.2 | loop fusion | flops 1310720 | bytes 6553600 | tf_op jit(solution)/shard_map/convert_element_type | solution.py:364
  (66 shorter events, 11.6 us)
Async XLA Ops:
  0.6 1.0 %copy-start.3 = (bf16[512,256]{1,0:T(8,128)(2,1)S(1)}, bf16[512,256]{1,0:T(8,128)(2,1)}, u32[]{:S(2)}) copy-start(bf16[512,256]{1,0:T(8,128)(2,1)} %left.1) | copy-start | bytes 786436
  1.6 0.9 %copy-start.4 = (bf16[512,256]{1,0:T(8,128)(2,1)S(1)}, bf16[512,256]{1,0:T(8,128)(2,1)}, u32[]{:S(2)}) copy-start(bf16[512,256]{1,0:T(8,128)(2,1)} %right.1) | copy-start | bytes 786436
  2.6 3.9 %collective-permute-start.1 = (bf16[512,512]{1,0:T(8,128)(2,1)S(1)}, bf16[512,512]{1,0:T(8,128)(2,1)S(1)}, u32[]{:S(2)}, u32[]{:S(2)}) collective-permute-start(bf16[512,512]{1,0:T(8,128)(2,1)S(1)} %shard_map.77.g0), channel_id=1, source_target_pairs={{0,1},{1,0},{2,3},{3,2},{4,5},{5,4},{6,7},{7,6},{8,9},{9,8},{10,11... | collective-permute-start | bytes 1572872 | tf_op jit(solution)/shard_map/ppermute | solution.py:58
  2.7 14.4 %collective-permute-start = (bf16[512,512]{1,0:T(8,128)(2,1)S(1)}, bf16[512,512]{1,0:T(8,128)(2,1)S(1)}, u32[]{:S(2)}, u32[]{:S(2)}) collective-permute-start(bf16[512,512]{1,0:T(8,128)(2,1)S(1)} %shard_map.77.g0), channel_id=1, source_target_pairs={{0,2},{1,3},{2,0},{3,1},{4,6},{5,7},{6,4},{7,5},{8,10},{9,11},{10,... | collective-permute-start | bytes 1572872 | tf_op jit(solution)/shard_map/ppermute | solution.py:58
  4.6 1.3 %copy-start.2 = (bf16[512,1280]{1,0:T(8,128)(2,1)S(1)}, bf16[512,1280]{1,0:T(8,128)(2,1)}, u32[]{:S(2)}) copy-start(bf16[512,1280]{1,0:T(8,128)(2,1)} %a_ref.1) | copy-start | bytes 3932164
  6.5 3.6 %copy-start.1 = (bf16[5120,256]{1,0:T(8,128)(2,1)S(1)}, bf16[5120,256]{1,0:T(8,128)(2,1)}, u32[]{:S(2)}) copy-start(bf16[5120,256]{1,0:T(8,128)(2,1)} %vw_ref) | copy-start | bytes 7864324
  8.4 1.7 %copy-start = (bf16[5120,256]{1,0:T(8,128)(2,1)S(1)}, bf16[5120,256]{1,0:T(8,128)(2,1)}, u32[]{:S(2)}) copy-start(bf16[5120,256]{1,0:T(8,128)(2,1)} %kw_ref) | copy-start | bytes 7864324
  8.5 12.6 %collective-permute-start.4 = (f16[656,512]{1,0:T(8,128)(2,1)S(1)}, f16[656,512]{1,0:T(8,128)(2,1)S(1)}, u32[]{:S(2)}, u32[]{:S(2)}) collective-permute-start(f16[656,512]{1,0:T(8,128)(2,1)S(1)} %convert_element_type.82), channel_id=1, source_target_pairs={{0,48},{1,13},{2,50},{3,15},{4,52},{5,9},{6,54},{7,11},{8,56},{9,5... | collective-permute-start | bytes 2015240 | tf_op jit(solution)/shard_map/ppermute | solution.py:58
  9.8 11.6 %collective-permute-start.3 = (f16[656,512]{1,0:T(8,128)(2,1)S(1)}, f16[656,512]{1,0:T(8,128)(2,1)S(1)}, u32[]{:S(2)}, u32[]{:S(2)}) collective-permute-start(f16[656,512]{1,0:T(8,128)(2,1)S(1)} %convert_element_type.81), channel_id=1, source_target_pairs={{0,16},{1,5},{2,18},{3,7},{4,20},{5,1},{6,22},{7,3},{8,24},{9,13},... | collective-permute-start | bytes 2015240 | tf_op jit(solution)/shard_map/ppermute | solution.py:58
  17.1 1.9 %collective-permute-start.2 = (bf16[512,512]{1,0:T(8,128)(2,1)S(1)}, bf16[512,512]{1,0:T(8,128)(2,1)S(1)}, u32[]{:S(2)}, u32[]{:S(2)}) collective-permute-start(bf16[512,512]{1,0:T(8,128)(2,1)S(1)} %collective-permute-done.g0), channel_id=1, source_target_pairs={{0,1},{1,0},{2,3},{3,2},{4,5},{5,4},{6,7},{7,6},{8,9},{9,8},{10,11... | collective-permute-start | bytes 1572872 | tf_op jit(solution)/shard_map/ppermute | solution.py:58
  17.1 8.3 %collective-permute-start.9 = (bf16[1280,512]{1,0:T(8,128)(2,1)S(1)}, bf16[1280,512]{1,0:T(8,128)(2,1)S(1)}, u32[]{:S(2)}, u32[]{:S(2)}) collective-permute-start(bf16[1280,512]{1,0:T(8,128)(2,1)S(1)} %get-tuple-element.100), channel_id=1, source_target_pairs={{0,1},{1,0},{2,3},{3,2},{4,5},{5,4},{6,7},{7,6},{8,9},{9,8},{10,11... | collective-permute-start | bytes 3932168 | tf_op jit(solution)/shard_map/ppermute | solution.py:58
  21.8 10.8 %collective-permute-start.5 = (f16[656,512]{1,0:T(8,128)(2,1)S(1)}, f16[656,512]{1,0:T(8,128)(2,1)S(1)}, u32[]{:S(2)}, u32[]{:S(2)}) collective-permute-start(f16[656,512]{1,0:T(8,128)(2,1)S(1)} %convert_element_type.83), channel_id=1, source_target_pairs={{0,16},{1,5},{2,18},{3,7},{4,20},{5,1},{6,22},{7,3},{8,24},{9,13},... | collective-permute-start | bytes 2015240 | tf_op jit(solution)/shard_map/ppermute | solution.py:58
  23.3 12.7 %collective-permute-start.7 = (f16[656,512]{1,0:T(8,128)(2,1)S(1)}, f16[656,512]{1,0:T(8,128)(2,1)S(1)}, u32[]{:S(2)}, u32[]{:S(2)}) collective-permute-start(f16[656,512]{1,0:T(8,128)(2,1)S(1)} %convert_element_type.84), channel_id=1, source_target_pairs={{0,48},{1,13},{2,50},{3,15},{4,52},{5,9},{6,54},{7,11},{8,56},{9,5... | collective-permute-start | bytes 2015240 | tf_op jit(solution)/shard_map/ppermute | solution.py:58
  25.4 36.1 %collective-permute-start.13 = (bf16[1280,512]{1,0:T(8,128)(2,1)S(1)}, bf16[1280,512]{1,0:T(8,128)(2,1)S(1)}, u32[]{:S(2)}, u32[]{:S(2)}) collective-permute-start(bf16[1280,512]{1,0:T(8,128)(2,1)S(1)} %get-tuple-element.116), channel_id=1, source_target_pairs={{0,194},{1,195},{2,64},{3,65},{4,198},{5,199},{6,68},{7,69},{8,202... | collective-permute-start | bytes 3932168 | tf_op jit(solution)/shard_map/ppermute | solution.py:58
  27.5 34.0 %collective-permute-start.14 = (bf16[1280,512]{1,0:T(8,128)(2,1)S(1)}, bf16[1280,512]{1,0:T(8,128)(2,1)S(1)}, u32[]{:S(2)}, u32[]{:S(2)}) collective-permute-start(bf16[1280,512]{1,0:T(8,128)(2,1)S(1)} %get-tuple-element.117), channel_id=1, source_target_pairs={{0,3},{1,2},{2,1},{3,0},{4,7},{5,6},{6,5},{7,4},{8,11},{9,10},{10,... | collective-permute-start | bytes 3932168 | tf_op jit(solution)/shard_map/ppermute | solution.py:58
  33.2 12.1 %collective-permute-start.6 = (f16[656,512]{1,0:T(8,128)(2,1)S(1)}, f16[656,512]{1,0:T(8,128)(2,1)S(1)}, u32[]{:S(2)}, u32[]{:S(2)}) collective-permute-start(f16[656,512]{1,0:T(8,128)(2,1)S(1)} %convert_element_type.88), channel_id=1, source_target_pairs={{0,48},{1,13},{2,50},{3,15},{4,52},{5,9},{6,54},{7,11},{8,56},{9,5... | collective-permute-start | bytes 2015240 | tf_op jit(solution)/shard_map/ppermute | solution.py:58
  36.6 11.0 %collective-permute-start.8 = (f16[656,512]{1,0:T(8,128)(2,1)S(1)}, f16[656,512]{1,0:T(8,128)(2,1)S(1)}, u32[]{:S(2)}, u32[]{:S(2)}) collective-permute-start(f16[656,512]{1,0:T(8,128)(2,1)S(1)} %convert_element_type.91), channel_id=1, source_target_pairs={{0,16},{1,5},{2,18},{3,7},{4,20},{5,1},{6,22},{7,3},{8,24},{9,13},... | collective-permute-start | bytes 2015240 | tf_op jit(solution)/shard_map/ppermute | solution.py:58
  48.3 12.2 %collective-permute-start.12 = (f16[336,512]{1,0:T(8,128)(2,1)S(1)}, f16[336,512]{1,0:T(8,128)(2,1)S(1)}, u32[]{:S(2)}, u32[]{:S(2)}) collective-permute-start(f16[336,512]{1,0:T(8,128)(2,1)S(1)} %convert_element_type.97), channel_id=1, source_target_pairs={{0,12},{1,49},{2,14},{3,51},{4,8},{5,53},{6,10},{7,55},{8,4},{9,57... | collective-permute-start | bytes 1032200 | tf_op jit(solution)/shard_map/ppermute | solution.py:58
  51.4 9.2 %collective-permute-start.11 = (f16[336,512]{1,0:T(8,128)(2,1)S(1)}, f16[336,512]{1,0:T(8,128)(2,1)S(1)}, u32[]{:S(2)}, u32[]{:S(2)}) collective-permute-start(f16[336,512]{1,0:T(8,128)(2,1)S(1)} %convert_element_type.95), channel_id=1, source_target_pairs={{0,8},{1,33},{2,10},{3,35},{4,12},{5,37},{6,14},{7,39},{8,0},{9,41... | collective-permute-start | bytes 1032200 | tf_op jit(solution)/shard_map/ppermute | solution.py:58
  52.1 9.4 %collective-permute-start.10 = (f16[336,512]{1,0:T(8,128)(2,1)S(1)}, f16[336,512]{1,0:T(8,128)(2,1)S(1)}, u32[]{:S(2)}, u32[]{:S(2)}) collective-permute-start(f16[336,512]{1,0:T(8,128)(2,1)S(1)} %convert_element_type.93), channel_id=1, source_target_pairs={{0,4},{1,17},{2,6},{3,19},{4,0},{5,21},{6,2},{7,23},{8,12},{9,25},... | collective-permute-start | bytes 1032200 | tf_op jit(solution)/shard_map/ppermute | solution.py:58
  61.9 17.1 %collective-permute-start.18 = (f16[176,256]{1,0:T(8,128)(2,1)S(1)}, f16[176,256]{1,0:T(8,128)(2,1)S(1)}, u32[]{:S(2)}, u32[]{:S(2)}) collective-permute-start(f16[176,256]{1,0:T(8,128)(2,1)S(1)} %convert_element_type.106), channel_id=1, source_target_pairs={{0,3},{1,67},{2,131},{3,195},{4,7},{5,71},{6,135},{7,199},{8,11},{... | collective-permute-start | bytes 270344 | tf_op jit(solution)/shard_map/ppermute | solution.py:58
  65.1 13.9 %collective-permute-start.17 = (f16[176,256]{1,0:T(8,128)(2,1)S(1)}, f16[176,256]{1,0:T(8,128)(2,1)S(1)}, u32[]{:S(2)}, u32[]{:S(2)}) collective-permute-start(f16[176,256]{1,0:T(8,128)(2,1)S(1)} %convert_element_type.104), channel_id=1, source_target_pairs={{0,2},{1,66},{2,130},{3,194},{4,6},{5,70},{6,134},{7,198},{8,10},{... | collective-permute-start | bytes 270344 | tf_op jit(solution)/shard_map/ppermute | solution.py:58
  68.4 10.7 %collective-permute-start.16 = (f16[176,256]{1,0:T(8,128)(2,1)S(1)}, f16[176,256]{1,0:T(8,128)(2,1)S(1)}, u32[]{:S(2)}, u32[]{:S(2)}) collective-permute-start(f16[176,256]{1,0:T(8,128)(2,1)S(1)} %convert_element_type.102), channel_id=1, source_target_pairs={{0,1},{1,65},{2,129},{3,193},{4,5},{5,69},{6,133},{7,197},{8,9},{9... | collective-permute-start | bytes 270344 | tf_op jit(solution)/shard_map/ppermute | solution.py:58
  68.4 10.7 %collective-permute-start.15 = (f16[176,256]{1,0:T(8,128)(2,1)S(1)}, f16[176,256]{1,0:T(8,128)(2,1)S(1)}, u32[]{:S(2)}, u32[]{:S(2)}) collective-permute-start(f16[176,256]{1,0:T(8,128)(2,1)S(1)} %convert_element_type.100), channel_id=1, source_target_pairs={{0,0},{1,64},{2,128},{3,192},{4,4},{5,68},{6,132},{7,196},{8,8},{9... | collective-permute-start | bytes 270344 | tf_op jit(solution)/shard_map/ppermute | solution.py:58
where the time goes:
time: 81.3 us; the launch traced here: 79.8 us
  starting transfers between devices  34.1 us (42%)
  waiting for transfers between devices  27.4 us (34%)
  Pallas kernels  6.96 us (9%)
  other arithmetic  3.57 us (4%)
  matrix products  3.51 us (4%)
  local copies, waits for them, and re-layouts  3.26 us (4%)
  between operations  1.03 us (1%)
    ppermute x19, starting transfers between devices, send(): return lax.ppermute(value, AXES, pairs)  34.1 us
    ppermute x19, waiting for transfers between devices, send(): return lax.ppermute(value, AXES, pairs)  27.4 us
    pallas_call x11, Pallas kernels, local_call(): pl.pallas_call(kernel, in_specs=specs or [VMEM] * len(operands), out_spec...  6.96 us
    dot_general x4, matrix products, right_product(): lax.dot_general(left, right, (((1,), (1,)), ((), ())), preferred_element_...  3.51 us
    unnamed x10, local copies, waits for them, and re-layouts  3.26 us
  transfers between devices with their start and end apart: 19, of which 7 were waited for; matrix products, arithmetic and copies ran while one was open for 9% of the time, Pallas kernels for 7%

commit v1 on v0

--- a/solution.py
+++ b/solution.py
@@ -153,37 +153,37 @@
     out[at : at + count, :] = jnp.broadcast_to(row, (count, out.shape[1]))
 
 
-def squares_kernel(at0, at1, g0, g1, keep0, bound0, out0, keep1, bound1, out1):
-    half, width = keep0.shape[0], g0.shape[1] // 2
-    step = half // 2
-    streams = ((at0, 0, keep0, bound0, out0), (at1, width, keep1, bound1, out1))
+def squares_kernel(moved, at0, at1, g0, g1, out0, bound0, out1, bound1):
+    half, width = at0.shape[0] // 2, g0.shape[1] // 2
+    step, base = half // 2, half if moved else 0
+    for at, lo, out, bound in ((at0, 0, out0, bound0), (at1, width, out1, bound1)):
+        tops = [jnp.zeros((8, width), jnp.float32)] * 2
+        for r in range(0, half, step):
+            rows = at[base + r : base + r + step, :]
+            for h, g in enumerate((g0, g1)):
+                grad = jnp.dot(rows, g[:, lo : lo + width], preferred_element_type=jnp.float32)
+                grad = grad * grad
+                out[r : r + step, h * width : (h + 1) * width] = grad
+                tops[h] = jnp.maximum(tops[h], jnp.max(grad.reshape(-1, 8, width), axis=0))
+        top = jnp.concatenate([jnp.max(top, axis=0, keepdims=True) for top in tops], axis=1)
+        bound[...] = top
+        if moved:
+            exponent = exponent_of(top)
+            scale = jnp.exp2(exponent)
+            for r in range(0, half, 80):
+                out[r : r + 80, :] = out[r : r + 80, :] * scale
+            fill(out, half, TAIL, exponent)
+
+
+def squares(at0, at1, g0, g1):
+    half, width = at0.shape[0] // 2, g0.shape[1]
+    both = []
     for moved in (True, False):
-        for at, lo, keep, bound, out in streams:
-            tops = [jnp.zeros((8, width), jnp.float32)] * 2
-            to, base = (out, half) if moved else (keep, 0)
-            for r in range(0, half, step):
-                rows = at[base + r : base + r + step, :]
-                for h, g in enumerate((g0, g1)):
-                    grad = jnp.dot(rows, g[:, lo : lo + width], preferred_element_type=jnp.float32)
-                    grad = grad * grad
-                    to[r : r + step, h * width : (h + 1) * width] = grad
-                    tops[h] = jnp.maximum(tops[h], jnp.max(grad.reshape(-1, 8, width), axis=0))
-            top = jnp.concatenate([jnp.max(top, axis=0, keepdims=True) for top in tops], axis=1)
-            if moved:
-                exponent = exponent_of(top)
-                scale = jnp.exp2(exponent)
-                for r in range(0, half, 80):
-                    out[r : r + 80, :] = out[r : r + 80, :] * scale
-                fill(out, half, TAIL, exponent)
-            else:
-                bound[...] = top
-
-
-def squares(at0, at1, g0, g1):
-    rows, width = at0.shape[0], g0.shape[1]
-    out = [shape(rows // 2, width), shape(1, width), shape(rows // 2 + TAIL, width)] * 2
-    out = local_call(squares_kernel, out, (at0, at1, g0, g1))
-    return out[:3], out[3:]
+        out = [shape(half + TAIL if moved else half, width), shape(1, width)] * 2
+        kernel = functools.partial(squares_kernel, moved)
+        both.append(local_call(kernel, out, (at0, at1, g0, g1)))
+    (out0, _, out1, _), (keep0, bound0, keep1, bound1) = both
+    return (keep0, bound0, out0), (keep1, bound1, out1)
 
 
 def add_kernel(keep0, bound0, got0, keep1, bound1, got1, sum0, top0, sum1, top1):

time: 81.3 us -> 81.2 us (level)
  waiting for transfers between devices: 27.4 us -> 25.8 us
  Pallas kernels: 6.96 us -> 8.45 us
    ppermute x19, waiting for transfers between devices: 27.4 us -> 25.8 us  [send(): return lax.ppermute(value, AXES, pairs)]
    pallas_call x11 -> x13, Pallas kernels: 6.96 us -> 8.45 us  [local_call(): pl.pallas_call(kernel, in_specs=specs or [VMEM] * len(operands), out_spec...]
  transfers between devices with their start and end apart: 19 -> 19, of which waited for: 7 -> 7; matrix products, arithmetic and copies ran while one was open for 9% -> 9% of each run, Pallas kernels for 7% -> 9%
where the time goes in v1:
time: 81.2 us; the launch traced here: 79.9 us
  starting transfers between devices  34.1 us (42%)
  waiting for transfers between devices  25.8 us (32%)
  Pallas kernels  8.45 us (10%)
  matrix products  3.61 us (4%)
  other arithmetic  3.58 us (4%)
  local copies, waits for them, and re-layouts  3.28 us (4%)
  between operations  1.01 us (1%)
    ppermute x19, starting transfers between devices, send(): return lax.ppermute(value, AXES, pairs)  34.1 us
    ppermute x19, waiting for transfers between devices, send(): return lax.ppermute(value, AXES, pairs)  25.8 us
    pallas_call x13, Pallas kernels, local_call(): pl.pallas_call(kernel, in_specs=specs or [VMEM] * len(operands), out_spec...  8.45 us
    dot_general x4, matrix products, right_product(): lax.dot_general(left, right, (((1,), (1,)), ((), ())), preferred_element_...  3.61 us
    unnamed x10, local copies, waits for them, and re-layouts  3.28 us
  transfers between devices with their start and end apart: 19, of which 7 were waited for; matrix products, arithmetic and copies ran while one was open for 9% of the time, Pallas kernels for 9%

profile of v1, /device:TPU:32, one launch (start us, length us, event | category | flops | bytes accessed | tf_op | source)
XLA Modules:
  0.0 79.9 jit_solution(11398712853660450026)
XLA Ops:
  0.6 0.9 %copy-done.3 = bf16[512,256]{1,0:T(8,128)(2,1)S(1)} copy-done((bf16[512,256]{1,0:T(8,128)(2,1)S(1)}, bf16[512,256]{1,0:T(8,128)(2,1)}, u32[]{:S(2)}) %copy-start.3) | copy-done | bytes 262168
  1.6 0.9 %copy-done.4 = bf16[512,256]{1,0:T(8,128)(2,1)S(1)} copy-done((bf16[512,256]{1,0:T(8,128)(2,1)S(1)}, bf16[512,256]{1,0:T(8,128)(2,1)}, u32[]{:S(2)}) %copy-start.4) | copy-done | bytes 262168
  2.7 1.9 %collective-permute-start = (bf16[512,512]{1,0:T(8,128)(2,1)S(1)}, bf16[512,512]{1,0:T(8,128)(2,1)S(1)}, u32[]{:S(2)}, u32[]{:S(2)}) collective-permute-start(bf16[512,512]{1,0:T(8,128)(2,1)S(1)} %shard_map.77.g0), channel_id=1, source_target_pairs={{0,2},{1,3},{2,0},{3,1},{4,6},{5,7},{6,4},{7,5},{8,10},{9,11},{10,... | collective-permute-start | bytes 1572872 | tf_op jit(solution)/shard_map/ppermute | solution.py:58
  4.6 1.3 %copy-done.2 = bf16[512,1280]{1,0:T(8,128)(2,1)S(1)} copy-done((bf16[512,1280]{1,0:T(8,128)(2,1)S(1)}, bf16[512,1280]{1,0:T(8,128)(2,1)}, u32[]{:S(2)}) %copy-start.2) | copy-done | bytes 1310744
  6.5 1.6 %shard_map.78 = (f32[656,512]{1,0:T(8,128)S(1)}, f32[1,512]{1,0:T(1,128)}, f32[656,512]{1,0:T(8,128)S(1)}, f32[1,512]{1,0:T(1,128)}) custom-call(bf16[1280,512]{1,0:T(8,128)(2,1)S(1)} %get-tuple-element.68.at0, bf16[1280,512]{1,0:T(8,128)(2,1)S(1)} %get-tuple-element.69.at1, bf16[512,512]{1,0:T(8,128)(2,1)S(1)} %shard_map.77.g0, ...), custom_call_target="tpu_custom_call" | custom-call | tf_op jit(solution)/shard_map/pallas_call | solution.py:62
  8.3 1.1 %collective-permute-start.4 = (f16[656,512]{1,0:T(8,128)(2,1)S(1)}, f16[656,512]{1,0:T(8,128)(2,1)S(1)}, u32[]{:S(2)}, u32[]{:S(2)}) collective-permute-start(f16[656,512]{1,0:T(8,128)(2,1)S(1)} %convert_element_type.82), channel_id=1, source_target_pairs={{0,48},{1,13},{2,50},{3,15},{4,52},{5,9},{6,54},{7,11},{8,56},{9,5... | collective-permute-start | bytes 2015240 | tf_op jit(solution)/shard_map/ppermute | solution.py:58
  10.4 6.7 %collective-permute-done.g0 = bf16[512,512]{1,0:T(8,128)(2,1)S(1)} collective-permute-done((bf16[512,512]{1,0:T(8,128)(2,1)S(1)}, bf16[512,512]{1,0:T(8,128)(2,1)S(1)}, u32[]{:S(2)}, u32[]{:S(2)}) %collective-permute-start) | collective-permute-done | bytes 524320 | tf_op jit(solution)/shard_map/ppermute | solution.py:58
  19.0 1.6 %shard_map.80 = (f32[656,512]{1,0:T(8,128)S(1)}, f32[1,512]{1,0:T(1,128)}, f32[656,512]{1,0:T(8,128)S(1)}, f32[1,512]{1,0:T(1,128)}) custom-call(bf16[1280,512]{1,0:T(8,128)(2,1)S(1)} %get-tuple-element.68.at0, bf16[1280,512]{1,0:T(8,128)(2,1)S(1)} %get-tuple-element.69.at1, bf16[512,512]{1,0:T(8,128)(2,1)S(1)} %collective-permute-done.g0, ...), custom_call_target="tpu_custom_call" | custom-call | tf_op jit(solution)/shard_map/pallas_call | solution.py:62
  21.7 1.5 %collective-permute-start.5 = (f16[656,512]{1,0:T(8,128)(2,1)S(1)}, f16[656,512]{1,0:T(8,128)(2,1)S(1)}, u32[]{:S(2)}, u32[]{:S(2)}) collective-permute-start(f16[656,512]{1,0:T(8,128)(2,1)S(1)} %convert_element_type.83), channel_id=1, source_target_pairs={{0,16},{1,5},{2,18},{3,7},{4,20},{5,1},{6,22},{7,3},{8,24},{9,13},... | collective-permute-start | bytes 2015240 | tf_op jit(solution)/shard_map/ppermute | solution.py:58
  23.2 2.1 %collective-permute-start.7 = (f16[656,512]{1,0:T(8,128)(2,1)S(1)}, f16[656,512]{1,0:T(8,128)(2,1)S(1)}, u32[]{:S(2)}, u32[]{:S(2)}) collective-permute-start(f16[656,512]{1,0:T(8,128)(2,1)S(1)} %convert_element_type.84), channel_id=1, source_target_pairs={{0,48},{1,13},{2,50},{3,15},{4,52},{5,9},{6,54},{7,11},{8,56},{9,5... | collective-permute-start | bytes 2015240 | tf_op jit(solution)/shard_map/ppermute | solution.py:58
  25.3 2.1 %collective-permute-start.13 = (bf16[1280,512]{1,0:T(8,128)(2,1)S(1)}, bf16[1280,512]{1,0:T(8,128)(2,1)S(1)}, u32[]{:S(2)}, u32[]{:S(2)}) collective-permute-start(bf16[1280,512]{1,0:T(8,128)(2,1)S(1)} %get-tuple-element.116), channel_id=1, source_target_pairs={{0,194},{1,195},{2,64},{3,65},{4,198},{5,199},{6,68},{7,69},{8,202... | collective-permute-start | bytes 3932168 | tf_op jit(solution)/shard_map/ppermute | solution.py:58
  27.4 3.0 %collective-permute-start.14 = (bf16[1280,512]{1,0:T(8,128)(2,1)S(1)}, bf16[1280,512]{1,0:T(8,128)(2,1)S(1)}, u32[]{:S(2)}, u32[]{:S(2)}) collective-permute-start(bf16[1280,512]{1,0:T(8,128)(2,1)S(1)} %get-tuple-element.117), channel_id=1, source_target_pairs={{0,3},{1,2},{2,1},{3,0},{4,7},{5,6},{6,5},{7,4},{8,11},{9,10},{10,... | collective-permute-start | bytes 3932168 | tf_op jit(solution)/shard_map/ppermute | solution.py:58
  31.2 1.4 %collective-permute-done.5 = f16[656,512]{1,0:T(8,128)(2,1)S(1)} collective-permute-done((f16[656,512]{1,0:T(8,128)(2,1)S(1)}, f16[656,512]{1,0:T(8,128)(2,1)S(1)}, u32[]{:S(2)}, u32[]{:S(2)}) %collective-permute-start.5) | collective-permute-done | bytes 671776 | tf_op jit(solution)/shard_map/ppermute | solution.py:58
  33.2 2.9 %collective-permute-start.6 = (f16[656,512]{1,0:T(8,128)(2,1)S(1)}, f16[656,512]{1,0:T(8,128)(2,1)S(1)}, u32[]{:S(2)}, u32[]{:S(2)}) collective-permute-start(f16[656,512]{1,0:T(8,128)(2,1)S(1)} %convert_element_type.88), channel_id=1, source_target_pairs={{0,48},{1,13},{2,50},{3,15},{4,52},{5,9},{6,54},{7,11},{8,56},{9,5... | collective-permute-start | bytes 2015240 | tf_op jit(solution)/shard_map/ppermute | solution.py:58
  37.9 0.9 %convolution_add_fusion.1 = f32[512,1280]{1,0:T(8,128)S(1)} fusion(f32[512,1280]{1,0:T(8,128)S(1)} %fusion, bf16[512,512]{1,0:T(8,128)(2,1)S(1)} %collective-permute-done.1.g1, bf16[1280,512]{1,0:T(8,128)(2,1)S(1)} %collective-permute-done.9), kind=kOutput, calls=%fused_computation.1 | convolution fusion | flops 671744000 | bytes 7077888 | tf_op jit(solution)/shard_map/dot_general | solution.py:311
  38.8 6.6 %collective-permute-done.6 = f16[656,512]{1,0:T(8,128)(2,1)S(1)} collective-permute-done((f16[656,512]{1,0:T(8,128)(2,1)S(1)}, f16[656,512]{1,0:T(8,128)(2,1)S(1)}, u32[]{:S(2)}, u32[]{:S(2)}) %collective-permute-start.6) | collective-permute-done | bytes 671776 | tf_op jit(solution)/shard_map/ppermute | solution.py:58
  45.6 2.0 %collective-permute-done.8 = f16[656,512]{1,0:T(8,128)(2,1)S(1)} collective-permute-done((f16[656,512]{1,0:T(8,128)(2,1)S(1)}, f16[656,512]{1,0:T(8,128)(2,1)S(1)}, u32[]{:S(2)}, u32[]{:S(2)}) %collective-permute-start.8) | collective-permute-done | bytes 671776 | tf_op jit(solution)/shard_map/ppermute | solution.py:58
  48.3 3.1 %collective-permute-start.12 = (f16[336,512]{1,0:T(8,128)(2,1)S(1)}, f16[336,512]{1,0:T(8,128)(2,1)S(1)}, u32[]{:S(2)}, u32[]{:S(2)}) collective-permute-start(f16[336,512]{1,0:T(8,128)(2,1)S(1)} %convert_element_type.97), channel_id=1, source_target_pairs={{0,12},{1,49},{2,14},{3,51},{4,8},{5,53},{6,10},{7,55},{8,4},{9,57... | collective-permute-start | bytes 1032200 | tf_op jit(solution)/shard_map/ppermute | solution.py:58
  52.6 7.9 %collective-permute-done.12 = f16[336,512]{1,0:T(8,128)(2,1)S(1)} collective-permute-done((f16[336,512]{1,0:T(8,128)(2,1)S(1)}, f16[336,512]{1,0:T(8,128)(2,1)S(1)}, u32[]{:S(2)}, u32[]{:S(2)}) %collective-permute-start.12) | collective-permute-done | bytes 344096 | tf_op jit(solution)/shard_map/ppermute | solution.py:58
  61.9 3.2 %collective-permute-start.18 = (f16[176,256]{1,0:T(8,128)(2,1)S(1)}, f16[176,256]{1,0:T(8,128)(2,1)S(1)}, u32[]{:S(2)}, u32[]{:S(2)}) collective-permute-start(f16[176,256]{1,0:T(8,128)(2,1)S(1)} %convert_element_type.106), channel_id=1, source_target_pairs={{0,3},{1,67},{2,131},{3,195},{4,7},{5,71},{6,135},{7,199},{8,11},{... | collective-permute-start | bytes 270344 | tf_op jit(solution)/shard_map/ppermute | solution.py:58
  65.1 3.2 %collective-permute-start.17 = (f16[176,256]{1,0:T(8,128)(2,1)S(1)}, f16[176,256]{1,0:T(8,128)(2,1)S(1)}, u32[]{:S(2)}, u32[]{:S(2)}) collective-permute-start(f16[176,256]{1,0:T(8,128)(2,1)S(1)} %convert_element_type.104), channel_id=1, source_target_pairs={{0,2},{1,66},{2,130},{3,194},{4,6},{5,70},{6,134},{7,198},{8,10},{... | collective-permute-start | bytes 270344 | tf_op jit(solution)/shard_map/ppermute | solution.py:58
  68.4 7.6 %collective-permute-start.15 = (f16[176,256]{1,0:T(8,128)(2,1)S(1)}, f16[176,256]{1,0:T(8,128)(2,1)S(1)}, u32[]{:S(2)}, u32[]{:S(2)}) collective-permute-start(f16[176,256]{1,0:T(8,128)(2,1)S(1)} %convert_element_type.100), channel_id=1, source_target_pairs={{0,0},{1,64},{2,128},{3,192},{4,4},{5,68},{6,132},{7,196},{8,8},{9... | collective-permute-start | bytes 270344 | tf_op jit(solution)/shard_map/ppermute | solution.py:58
  76.8 0.9 %convolution_add_fusion = f32[512,1280]{1,0:T(8,128)S(1)} fusion(f32[512,1280]{1,0:T(8,128)S(1)} %fusion.1, bf16[512,512]{1,0:T(8,128)(2,1)S(1)} %collective-permute-done.g0, bf16[1280,512]{1,0:T(8,128)(2,1)S(1)} %collective-permute-done.13), kind=kOutput, calls=%fused_computation | convolution fusion | flops 671744000 | bytes 7077888 | tf_op jit(solution)/shard_map/dot_general | solution.py:311
  77.8 1.3 %add_convert_fusion = bf16[512,1280]{1,0:T(8,128)(2,1)} fusion(f32[512,1280]{1,0:T(8,128)S(1)} %convolution_add_fusion.1, f32[512,1280]{1,0:T(8,128)S(1)} %convolution_add_fusion), kind=kLoop, calls=%fused_computation.2 | loop fusion | flops 1310720 | bytes 6553600 | tf_op jit(solution)/shard_map/convert_element_type | solution.py:364
  (68 shorter events, 13.0 us)
Async XLA Ops:
  0.6 1.0 %copy-start.3 = (bf16[512,256]{1,0:T(8,128)(2,1)S(1)}, bf16[512,256]{1,0:T(8,128)(2,1)}, u32[]{:S(2)}) copy-start(bf16[512,256]{1,0:T(8,128)(2,1)} %left.1) | copy-start | bytes 786436
  1.6 0.9 %copy-start.4 = (bf16[512,256]{1,0:T(8,128)(2,1)S(1)}, bf16[512,256]{1,0:T(8,128)(2,1)}, u32[]{:S(2)}) copy-start(bf16[512,256]{1,0:T(8,128)(2,1)} %right.1) | copy-start | bytes 786436
  2.6 3.9 %collective-permute-start.1 = (bf16[512,512]{1,0:T(8,128)(2,1)S(1)}, bf16[512,512]{1,0:T(8,128)(2,1)S(1)}, u32[]{:S(2)}, u32[]{:S(2)}) collective-permute-start(bf16[512,512]{1,0:T(8,128)(2,1)S(1)} %shard_map.77.g0), channel_id=1, source_target_pairs={{0,1},{1,0},{2,3},{3,2},{4,5},{5,4},{6,7},{7,6},{8,9},{9,8},{10,11... | collective-permute-start | bytes 1572872 | tf_op jit(solution)/shard_map/ppermute | solution.py:58
  2.7 14.4 %collective-permute-start = (bf16[512,512]{1,0:T(8,128)(2,1)S(1)}, bf16[512,512]{1,0:T(8,128)(2,1)S(1)}, u32[]{:S(2)}, u32[]{:S(2)}) collective-permute-start(bf16[512,512]{1,0:T(8,128)(2,1)S(1)} %shard_map.77.g0), channel_id=1, source_target_pairs={{0,2},{1,3},{2,0},{3,1},{4,6},{5,7},{6,4},{7,5},{8,10},{9,11},{10,... | collective-permute-start | bytes 1572872 | tf_op jit(solution)/shard_map/ppermute | solution.py:58
  4.6 1.3 %copy-start.2 = (bf16[512,1280]{1,0:T(8,128)(2,1)S(1)}, bf16[512,1280]{1,0:T(8,128)(2,1)}, u32[]{:S(2)}) copy-start(bf16[512,1280]{1,0:T(8,128)(2,1)} %a_ref.1) | copy-start | bytes 3932164
  6.5 3.3 %copy-start.1 = (bf16[5120,256]{1,0:T(8,128)(2,1)S(1)}, bf16[5120,256]{1,0:T(8,128)(2,1)}, u32[]{:S(2)}) copy-start(bf16[5120,256]{1,0:T(8,128)(2,1)} %vw_ref) | copy-start | bytes 7864324
  8.2 1.8 %copy-start = (bf16[5120,256]{1,0:T(8,128)(2,1)S(1)}, bf16[5120,256]{1,0:T(8,128)(2,1)}, u32[]{:S(2)}) copy-start(bf16[5120,256]{1,0:T(8,128)(2,1)} %kw_ref) | copy-start | bytes 7864324
  8.3 12.6 %collective-permute-start.4 = (f16[656,512]{1,0:T(8,128)(2,1)S(1)}, f16[656,512]{1,0:T(8,128)(2,1)S(1)}, u32[]{:S(2)}, u32[]{:S(2)}) collective-permute-start(f16[656,512]{1,0:T(8,128)(2,1)S(1)} %convert_element_type.82), channel_id=1, source_target_pairs={{0,48},{1,13},{2,50},{3,15},{4,52},{5,9},{6,54},{7,11},{8,56},{9,5... | collective-permute-start | bytes 2015240 | tf_op jit(solution)/shard_map/ppermute | solution.py:58
  9.6 11.6 %collective-permute-start.3 = (f16[656,512]{1,0:T(8,128)(2,1)S(1)}, f16[656,512]{1,0:T(8,128)(2,1)S(1)}, u32[]{:S(2)}, u32[]{:S(2)}) collective-permute-start(f16[656,512]{1,0:T(8,128)(2,1)S(1)} %convert_element_type.81), channel_id=1, source_target_pairs={{0,16},{1,5},{2,18},{3,7},{4,20},{5,1},{6,22},{7,3},{8,24},{9,13},... | collective-permute-start | bytes 2015240 | tf_op jit(solution)/shard_map/ppermute | solution.py:58
  17.1 1.9 %collective-permute-start.2 = (bf16[512,512]{1,0:T(8,128)(2,1)S(1)}, bf16[512,512]{1,0:T(8,128)(2,1)S(1)}, u32[]{:S(2)}, u32[]{:S(2)}) collective-permute-start(bf16[512,512]{1,0:T(8,128)(2,1)S(1)} %collective-permute-done.g0), channel_id=1, source_target_pairs={{0,1},{1,0},{2,3},{3,2},{4,5},{5,4},{6,7},{7,6},{8,9},{9,8},{10,11... | collective-permute-start | bytes 1572872 | tf_op jit(solution)/shard_map/ppermute | solution.py:58
  17.1 8.2 %collective-permute-start.9 = (bf16[1280,512]{1,0:T(8,128)(2,1)S(1)}, bf16[1280,512]{1,0:T(8,128)(2,1)S(1)}, u32[]{:S(2)}, u32[]{:S(2)}) collective-permute-start(bf16[1280,512]{1,0:T(8,128)(2,1)S(1)} %get-tuple-element.100), channel_id=1, source_target_pairs={{0,1},{1,0},{2,3},{3,2},{4,5},{5,4},{6,7},{7,6},{8,9},{9,8},{10,11... | collective-permute-start | bytes 3932168 | tf_op jit(solution)/shard_map/ppermute | solution.py:58
  21.7 10.8 %collective-permute-start.5 = (f16[656,512]{1,0:T(8,128)(2,1)S(1)}, f16[656,512]{1,0:T(8,128)(2,1)S(1)}, u32[]{:S(2)}, u32[]{:S(2)}) collective-permute-start(f16[656,512]{1,0:T(8,128)(2,1)S(1)} %convert_element_type.83), channel_id=1, source_target_pairs={{0,16},{1,5},{2,18},{3,7},{4,20},{5,1},{6,22},{7,3},{8,24},{9,13},... | collective-permute-start | bytes 2015240 | tf_op jit(solution)/shard_map/ppermute | solution.py:58
  23.2 12.9 %collective-permute-start.7 = (f16[656,512]{1,0:T(8,128)(2,1)S(1)}, f16[656,512]{1,0:T(8,128)(2,1)S(1)}, u32[]{:S(2)}, u32[]{:S(2)}) collective-permute-start(f16[656,512]{1,0:T(8,128)(2,1)S(1)} %convert_element_type.84), channel_id=1, source_target_pairs={{0,48},{1,13},{2,50},{3,15},{4,52},{5,9},{6,54},{7,11},{8,56},{9,5... | collective-permute-start | bytes 2015240 | tf_op jit(solution)/shard_map/ppermute | solution.py:58
  25.3 36.2 %collective-permute-start.13 = (bf16[1280,512]{1,0:T(8,128)(2,1)S(1)}, bf16[1280,512]{1,0:T(8,128)(2,1)S(1)}, u32[]{:S(2)}, u32[]{:S(2)}) collective-permute-start(bf16[1280,512]{1,0:T(8,128)(2,1)S(1)} %get-tuple-element.116), channel_id=1, source_target_pairs={{0,194},{1,195},{2,64},{3,65},{4,198},{5,199},{6,68},{7,69},{8,202... | collective-permute-start | bytes 3932168 | tf_op jit(solution)/shard_map/ppermute | solution.py:58
  27.4 34.1 %collective-permute-start.14 = (bf16[1280,512]{1,0:T(8,128)(2,1)S(1)}, bf16[1280,512]{1,0:T(8,128)(2,1)S(1)}, u32[]{:S(2)}, u32[]{:S(2)}) collective-permute-start(bf16[1280,512]{1,0:T(8,128)(2,1)S(1)} %get-tuple-element.117), channel_id=1, source_target_pairs={{0,3},{1,2},{2,1},{3,0},{4,7},{5,6},{6,5},{7,4},{8,11},{9,10},{10,... | collective-permute-start | bytes 3932168 | tf_op jit(solution)/shard_map/ppermute | solution.py:58
  33.2 12.2 %collective-permute-start.6 = (f16[656,512]{1,0:T(8,128)(2,1)S(1)}, f16[656,512]{1,0:T(8,128)(2,1)S(1)}, u32[]{:S(2)}, u32[]{:S(2)}) collective-permute-start(f16[656,512]{1,0:T(8,128)(2,1)S(1)} %convert_element_type.88), channel_id=1, source_target_pairs={{0,48},{1,13},{2,50},{3,15},{4,52},{5,9},{6,54},{7,11},{8,56},{9,5... | collective-permute-start | bytes 2015240 | tf_op jit(solution)/shard_map/ppermute | solution.py:58
  36.7 10.8 %collective-permute-start.8 = (f16[656,512]{1,0:T(8,128)(2,1)S(1)}, f16[656,512]{1,0:T(8,128)(2,1)S(1)}, u32[]{:S(2)}, u32[]{:S(2)}) collective-permute-start(f16[656,512]{1,0:T(8,128)(2,1)S(1)} %convert_element_type.91), channel_id=1, source_target_pairs={{0,16},{1,5},{2,18},{3,7},{4,20},{5,1},{6,22},{7,3},{8,24},{9,13},... | collective-permute-start | bytes 2015240 | tf_op jit(solution)/shard_map/ppermute | solution.py:58
  48.3 12.2 %collective-permute-start.12 = (f16[336,512]{1,0:T(8,128)(2,1)S(1)}, f16[336,512]{1,0:T(8,128)(2,1)S(1)}, u32[]{:S(2)}, u32[]{:S(2)}) collective-permute-start(f16[336,512]{1,0:T(8,128)(2,1)S(1)} %convert_element_type.97), channel_id=1, source_target_pairs={{0,12},{1,49},{2,14},{3,51},{4,8},{5,53},{6,10},{7,55},{8,4},{9,57... | collective-permute-start | bytes 1032200 | tf_op jit(solution)/shard_map/ppermute | solution.py:58
  51.4 9.2 %collective-permute-start.11 = (f16[336,512]{1,0:T(8,128)(2,1)S(1)}, f16[336,512]{1,0:T(8,128)(2,1)S(1)}, u32[]{:S(2)}, u32[]{:S(2)}) collective-permute-start(f16[336,512]{1,0:T(8,128)(2,1)S(1)} %convert_element_type.95), channel_id=1, source_target_pairs={{0,8},{1,33},{2,10},{3,35},{4,12},{5,37},{6,14},{7,39},{8,0},{9,41... | collective-permute-start | bytes 1032200 | tf_op jit(solution)/shard_map/ppermute | solution.py:58
  52.0 9.4 %collective-permute-start.10 = (f16[336,512]{1,0:T(8,128)(2,1)S(1)}, f16[336,512]{1,0:T(8,128)(2,1)S(1)}, u32[]{:S(2)}, u32[]{:S(2)}) collective-permute-start(f16[336,512]{1,0:T(8,128)(2,1)S(1)} %convert_element_type.93), channel_id=1, source_target_pairs={{0,4},{1,17},{2,6},{3,19},{4,0},{5,21},{6,2},{7,23},{8,12},{9,25},... | collective-permute-start | bytes 1032200 | tf_op jit(solution)/shard_map/ppermute | solution.py:58
  61.9 17.2 %collective-permute-start.18 = (f16[176,256]{1,0:T(8,128)(2,1)S(1)}, f16[176,256]{1,0:T(8,128)(2,1)S(1)}, u32[]{:S(2)}, u32[]{:S(2)}) collective-permute-start(f16[176,256]{1,0:T(8,128)(2,1)S(1)} %convert_element_type.106), channel_id=1, source_target_pairs={{0,3},{1,67},{2,131},{3,195},{4,7},{5,71},{6,135},{7,199},{8,11},{... | collective-permute-start | bytes 270344 | tf_op jit(solution)/shard_map/ppermute | solution.py:58
  65.1 13.9 %collective-permute-start.17 = (f16[176,256]{1,0:T(8,128)(2,1)S(1)}, f16[176,256]{1,0:T(8,128)(2,1)S(1)}, u32[]{:S(2)}, u32[]{:S(2)}) collective-permute-start(f16[176,256]{1,0:T(8,128)(2,1)S(1)} %convert_element_type.104), channel_id=1, source_target_pairs={{0,2},{1,66},{2,130},{3,194},{4,6},{5,70},{6,134},{7,198},{8,10},{... | collective-permute-start | bytes 270344 | tf_op jit(solution)/shard_map/ppermute | solution.py:58
  68.4 10.8 %collective-permute-start.16 = (f16[176,256]{1,0:T(8,128)(2,1)S(1)}, f16[176,256]{1,0:T(8,128)(2,1)S(1)}, u32[]{:S(2)}, u32[]{:S(2)}) collective-permute-start(f16[176,256]{1,0:T(8,128)(2,1)S(1)} %convert_element_type.102), channel_id=1, source_target_pairs={{0,1},{1,65},{2,129},{3,193},{4,5},{5,69},{6,133},{7,197},{8,9},{9... | collective-permute-start | bytes 270344 | tf_op jit(solution)/shard_map/ppermute | solution.py:58
  68.4 10.8 %collective-permute-start.15 = (f16[176,256]{1,0:T(8,128)(2,1)S(1)}, f16[176,256]{1,0:T(8,128)(2,1)S(1)}, u32[]{:S(2)}, u32[]{:S(2)}) collective-permute-start(f16[176,256]{1,0:T(8,128)(2,1)S(1)} %convert_element_type.100), channel_id=1, source_target_pairs={{0,0},{1,64},{2,128},{3,192},{4,4},{5,68},{6,132},{7,196},{8,8},{9... | collective-permute-start | bytes 270344 | tf_op jit(solution)/shard_map/ppermute | solution.py:58
